TPU v7x, 32 devices: a whole 2x2x4 slice. The times are simulated.
32 devices in a mesh: gx: 8 (over z, y), gy: 2 (over x), gz: 2 (over core).
Axes of the slice: x: 2, y: 2, z: 4, core: 2. Of those that a mesh axis runs over, the one named last changes fastest.
Arguments:
- dual_result_fields: float32 [5, 64, 32, 512], P(None, 'gx', 'gy', 'gz'), may hold values from -24 to 24, as said below
- scaled_mass_per_volume: float32 [64, 32, 512], P('gx', 'gy', 'gz'), may hold values from 0.2 to 2.5
- scaled_thermal_level: float32 [64, 32, 512], P('gx', 'gy', 'gz'), may hold values from 0.6 to 2
- interaction_matrix: float32 [5, 5], replicated, may hold values from -2 to 2
Outputs:
- adjoint_prior: float32 [5, 64, 32, 512], P(None, 'gx', 'gy', 'gz')
Inputs may be any that keep to these rules, and one draw needn't show every extreme that they name: `dual_result_fields`: finite values.
All inputs are finite; a program needn't handle non-finite values.
Results may differ from a plain program's by a relative error of at most 0.00026.
Values sent between devices are 32-bit elements; how exact they have to be, the bound alone decides.
A program may use at most 64 MiB of HBM per device.

v0:
```python
import math

import jax
import jax.numpy as jnp
from jax import lax
from jax.sharding import PartitionSpec as P


def entering(value, axis, join, neutral, backward):
    count, mine = (lax.axis_size(axis), lax.axis_index(axis))
    pieces = jax.tree.map(lambda part: lax.all_gather(part, axis), value)
    if backward:
        pieces = jax.tree.map(lambda part: part[::-1], pieces)
        mine = count - 1 - mine
    running = jax.tree.map(
        lambda part, zero: jnp.full_like(part, 0) + jnp.asarray(zero, part.dtype), value, neutral
    )

    def lap(position, running):
        longer = join(running, jax.tree.map(lambda part: part[position], pieces))
        return jax.tree.map(lambda new, old: jnp.where(position < mine, new, old), longer, running)

    return lax.fori_loop(0, count - 1, lap, running)


def padded_2(block, sides, width, periodic):
    for axis, dim in sides:
        count = lax.axis_size(axis)
        forward = [(i, i + 1) for i in range(count - 1)]
        if periodic:
            forward.append((count - 1, 0))
        backward = [(target, source) for source, target in forward]
        low = lax.ppermute(
            lax.slice_in_dim(block, block.shape[dim] - width, None, axis=dim), axis, forward
        )
        high = lax.ppermute(lax.slice_in_dim(block, 0, width, axis=dim), axis, backward)
        block = jnp.concatenate([low, block, high], axis=dim)
    return block


def line_constants(total_cells):
    stiffness = total_cells * total_cells / 4.0
    decay_rate = 1.0 + 0.5 / stiffness - math.sqrt((1.0 + 0.5 / stiffness) ** 2 - 1.0)
    return (decay_rate, stiffness / decay_rate)


def central(padded, axis, length):

    def shifted(offset):
        return lax.slice_in_dim(padded, 3 + offset, 3 + offset + length, axis=axis)

    return (
        0.75 * (shifted(1) - shifted(-1))
        - 0.15 * (shifted(2) - shifted(-2))
        + (shifted(3) - shifted(-3)) / 60.0
    )


def pressure_wave_celerity(scaled_mass_per_volume, scaled_thermal_level):
    cohesion_pressure_part = 1.5 * (1.0 + 0.392 * (1.0 - jnp.sqrt(scaled_thermal_level))) ** 2
    divisor_quantity = (
        1.0
        + 0.5 * scaled_mass_per_volume
        - 0.0625 * scaled_mass_per_volume * scaled_mass_per_volume
    )
    return scaled_thermal_level / (
        1.0 - 0.25 * scaled_mass_per_volume
    ) ** 2 - cohesion_pressure_part * (
        2.0 * scaled_mass_per_volume * divisor_quantity
        - scaled_mass_per_volume * scaled_mass_per_volume * (0.5 - 0.125 * scaled_mass_per_volume)
    ) / (
        divisor_quantity * divisor_quantity
    )


def chain_step(first_part, second_part):
    return (first_part[0] * second_part[0], second_part[0] * first_part[1] + second_part[1])


def forward_sweep(source, decay_rate):
    length = source.shape[1]
    count_x = lax.axis_size("gx")
    device = lax.axis_index("gx")
    running = jnp.zeros_like(source[:, 0])
    values_list = []
    for position in range(length):
        running = source[:, position] + decay_rate * running
        values_list.append(running)
    last_row = values_list[-1]
    power_term = jnp.full((1, 1, 1), decay_rate**length, jnp.float32)
    prior_scale, prior_value = entering(
        (power_term, last_row),
        "gx",
        chain_step,
        (jnp.ones_like(power_term), jnp.zeros_like(last_row)),
        False,
    )
    weight = jnp.power(jnp.float32(decay_rate**length), (count_x - 1 - device).astype(jnp.float32))
    wrapped = lax.psum(weight * last_row, "gx")
    incoming = prior_value + prior_scale * (wrapped / (1.0 - decay_rate ** (length * count_x)))
    return jnp.stack(
        [
            values_list[position] + decay_rate ** (position + 1) * incoming
            for position in range(length)
        ],
        axis=1,
    )


def backward_sweep(source, decay_rate):
    length = source.shape[1]
    count_x = lax.axis_size("gx")
    device = lax.axis_index("gx")
    running = jnp.zeros_like(source[:, 0])
    values_list = [None] * length
    for position in range(length - 1, -1, -1):
        running = source[:, position] + decay_rate * running
        values_list[position] = running
    first_row = values_list[0]
    power_term = jnp.full((1, 1, 1), decay_rate**length, jnp.float32)
    prior_scale, prior_value = entering(
        (power_term, first_row),
        "gx",
        chain_step,
        (jnp.ones_like(power_term), jnp.zeros_like(first_row)),
        True,
    )
    weight = jnp.power(jnp.float32(decay_rate**length), device.astype(jnp.float32))
    wrapped = lax.psum(weight * first_row, "gx")
    incoming = prior_value + prior_scale * (wrapped / (1.0 - decay_rate ** (length * count_x)))
    return jnp.stack(
        [
            values_list[position] + decay_rate ** (length - position) * incoming
            for position in range(length)
        ],
        axis=1,
    )


def per_device(
    dual_result_fields, scaled_mass_per_volume, scaled_thermal_level, interaction_matrix
):
    decay_rate, factor = line_constants(dual_result_fields.shape[1] * lax.axis_size("gx"))
    implicit = backward_sweep(forward_sweep(dual_result_fields, decay_rate), decay_rate) / factor
    wave_celerity_factor = pressure_wave_celerity(scaled_mass_per_volume, scaled_thermal_level)
    padded_y = padded_2(implicit, (("gy", 2),), 3, False)
    padded_z = padded_2(implicit, (("gz", 3),), 3, True)
    slopes = central(padded_y, 2, implicit.shape[2]) + central(padded_z, 3, implicit.shape[3])
    coupled = jnp.einsum(
        "kj,kxyz->jxyz", interaction_matrix, slopes, precision=lax.Precision.HIGHEST
    )
    return implicit + wave_celerity_factor[None] * coupled


def solution(mesh):
    in_specs = (P(None, "gx", "gy", "gz"), P("gx", "gy", "gz"), P("gx", "gy", "gz"), P())
    out_specs = P(None, "gx", "gy", "gz")
    return jax.shard_map(
        per_device, mesh=mesh, in_specs=in_specs, out_specs=out_specs, check_vma=False
    )
```

profile of v0, /device:TPU:0, one launch (start us, length us, event | category | flops | bytes accessed | tf_op | source)
XLA Modules:
  0.0 179.6 jit_solution(16310146999248459993)
XLA Ops:
  6.5 1.2 fusion.74
  7.8 1.1 fusion.64
  9.4 0.7 dynamic-slice
  10.1 0.8 dynamic-update-slice
  10.9 23.1 %all-reduce = f32[8]{0:T(128)S(1)} all-reduce(f32[8]{0:T(128)S(1)} %dynamic-update-slice), channel_id=1, replica_groups=mesh['gx'=8,'gy'=2,'gz'=2] {'gx'}, use_global_device_ids=true, to_apply=%add | all-reduce | flops 8 | bytes 64
  34.0 32.0 %all_gather.15 = f32[8,5,16,256]{3,2,1,0:T(8,128)S(1)} all-gather(f32[1,5,16,256]{3,2,1,0:T(8,128)S(1)} %copy.45), channel_id=1, replica_groups=mesh['gx'=8,'gy'=2,'gz'=2] {'gx'}, dimensions={0}, use_global_device_ids=true | all-gather | bytes 737280 | tf_op jit(solution)/shard_map/all_gather | solution.py:11
  66.0 12.5 %while.32 = (s32[]{:T(128)}, f32[1,1,1]{2,1,0:T(1,128)}, f32[5,16,256]{2,1,0:T(8,128)S(1)}, s32[]{:T(128)}, f32[8,1,1,1]{0,3,2,1:T(1,128)S(1)}, /*index=5*/f32[8,5,16,256]{3,2,1,0:T(8,128)S(1)}, s32[]{:T(128)}, s32[]{:T(128)}) while((s32[]{:T(128)}, f32[1,1,1]{2,1,0:T(1,128)}, f32[5,16,256]{2,1,0:T(8,128)S(1)}, s32[]{:T(128)}, ...), condition=%wide.region_1.2_spmd.clone, body=%wide.region_0.1_spmd.clone.sunk | while | flops 81926 | bytes 245918 | solution.py:23
  66.0 0.6 constant_dynamic-slice_fusion.4
  67.2 0.6 fusion.77
  67.8 0.6 constant_dynamic-slice_fusion.4
  69.0 0.6 fusion.77
  69.6 0.6 constant_dynamic-slice_fusion.4
  70.8 0.6 fusion.77
  71.4 0.6 constant_dynamic-slice_fusion.4
  72.6 0.6 fusion.77
  73.2 0.6 constant_dynamic-slice_fusion.4
  74.4 0.6 fusion.77
  75.0 0.6 constant_dynamic-slice_fusion.4
  76.2 0.6 fusion.77
  76.8 0.6 constant_dynamic-slice_fusion.4
  78.0 0.6 fusion.77
  78.7 4.4 %all-reduce.4.cloned.1.call-done = f32[5,16,256]{2,0,1:T(8,128)} async-done(((f32[5,16,256]{2,0,1:T(8,128)}), f32[5,16,256]{2,0,1:T(8,128)}) %all-reduce.4.cloned.1.call-update) | async-done | bytes 81936 | tf_op jit(solution)/shard_map/psum | solution.py:99
  83.1 2.1 %broadcast_multiply_fusion.1 = (f32[5,16,256]{2,0,1:T(8,128)}, f32[5,16,256]{2,0,1:T(8,128)S(1)}, f32[5,16,256]{2,0,1:T(8,128)S(1)}, f32[5,16,256]{2,0,1:T(8,128)S(1)}, f32[5,16,256]{2,0,1:T(8,128)S(1)}) fusion(f32[]{:T(128)S(6)} %pow.7, f32[5,1,16,256]{3,2,1,0:T(8,128)S(1)} %get-tuple-element.351, f32[5,1,16,256]{3,2,1,0:T(8,128)S(1)} %get-tuple-element.350, ...), kind=kLoop, calls=%fused_computation.116 | loop fusion | flops 921600 | bytes 1228808 | tf_op jit(solution)/shard_map/mul | solution.py:129
  85.3 31.9 %all-gather = f32[40,16,256]{2,1,0:T(8,128)S(1)} all-gather(f32[5,16,256]{2,1,0:T(8,128)S(1)} %copy.48), channel_id=2, replica_groups=mesh['gx'=8,'gy'=2,'gz'=2] {'gx'}, dimensions={0}, use_global_device_ids=true | all-gather | bytes 737280 | tf_op jit(solution)/shard_map/all_gather | solution.py:11
  117.3 14.8 %while.33 = (s32[]{:T(128)}, f32[1,1,1]{2,1,0:T(1,128)}, f32[5,16,256]{2,1,0:T(8,128)S(1)}, s32[]{:T(128)}, f32[8,1,1,1]{0,3,2,1:T(1,128)S(1)}, /*index=5*/f32[8,5,16,256]{3,2,1,0:T(8,128)S(1)}, s32[]{:T(128)}, s32[]{:T(128)}) while((s32[]{:T(128)}, f32[1,1,1]{2,1,0:T(1,128)}, f32[5,16,256]{2,1,0:T(8,128)S(1)}, s32[]{:T(128)}, ...), condition=%wide.region_4.5_spmd.clone, body=%wide.region_3.4_spmd.clone.sunk | while | flops 81926 | bytes 245918 | solution.py:23
  117.3 0.7 constant_dynamic-slice_fusion.5
  118.7 0.7 fusion.78
  119.4 0.7 constant_dynamic-slice_fusion.5
  120.8 0.7 fusion.78
  121.5 0.7 constant_dynamic-slice_fusion.5
  122.9 0.7 fusion.78
  123.6 0.7 constant_dynamic-slice_fusion.5
  125.0 0.7 fusion.78
  125.7 0.7 constant_dynamic-slice_fusion.5
  127.1 0.7 fusion.78
  127.9 0.7 constant_dynamic-slice_fusion.5
  129.2 0.7 fusion.78
  130.0 0.7 constant_dynamic-slice_fusion.5
  131.3 0.7 fusion.78
  132.1 23.9 %all-reduce.6.cloned.1.call-done = f32[5,16,256]{2,0,1:T(8,128)} async-done(((f32[5,16,256]{2,0,1:T(8,128)}), f32[5,16,256]{2,0,1:T(8,128)}) %all-reduce.6.cloned.1.call-update) | async-done | bytes 81936 | tf_op jit(solution)/shard_map/psum | solution.py:129
  155.9 1.0 bitcast_dynamic-update-slice_fusion.7
  158.4 1.3 collective-permute-start
  159.7 4.6 %collective-permute-start.1 = (f32[5,8,3,256]{3,0,2,1:T(8,128)S(1)}, f32[5,8,3,256]{3,0,2,1:T(8,128)S(1)}, u32[]{:S(2)}, u32[]{:S(2)}) collective-permute-start(f32[5,8,3,256]{3,0,2,1:T(8,128)S(1)} %get-tuple-element.343), channel_id=1, source_target_pairs={{0,2},{1,3},{4,6},{5,7},{8,10},{9,11},{12,14},{13,15},{16,18},{17,... | collective-permute-start | bytes 368648 | tf_op jit(solution)/shard_map/ppermute | solution.py:33
  164.4 0.5 collective-permute-start.3
  165.0 1.2 collective-permute-done.2
  166.3 0.7 collective-permute-done.3
  167.5 4.3 %fusion.3 = f32[5,8,16,256]{3,0,2,1:T(8,128)S(1)} fusion(f32[5,8,16,256]{3,0,2,1:T(8,128)S(1)} %broadcast_multiply_fusion, f32[5,8,3,256]{3,0,2,1:T(8,128)S(1)} %collective-permute-done.1, f32[5,8,3,256]{3,0,2,1:T(8,128)S(1)} %collective-permute-done, f32[5,8,16,3]{3,0,2,1:T(8,128)S(1)} %collective-permute-done.3, ...), kind=kOutput, calls=%fused_computation.20 | convolution fusion | flops 14909440 | bytes 4329472 | tf_op jit(solution)/shard_map/kj,kxyz->jxyz/dot_general | solution.py:149
  171.7 1.0 copy.52
  (34 shorter events, 2.8 us)
Async XLA Ops:
  6.5 160.9 %copy-start = (f32[5,5]{1,0:T(8,128)S(1)}, f32[5,5]{1,0:T(8,128)}, u32[]{:S(2)}) copy-start(f32[5,5]{1,0:T(8,128)} %param.11) | copy-start | bytes 304
  6.5 76.6 %all-reduce.4.cloned.1.call-start = ((), (), s32[]{:S(2)}) async-start(), calls=%async_computation | async-start | bytes 262144 | tf_op jit(solution)/shard_map/psum | solution.py:99
  7.8 1.6 copy-start.3
  8.9 147.0 %all-reduce.6.cloned.1.call-start = ((), (), s32[]{:S(2)}) async-start(), calls=%async_computation.1 | async-start | bytes 262144 | tf_op jit(solution)/shard_map/psum | solution.py:129
  158.2 6.7 %copy-start.1 = (f32[8,16,256]{2,1,0:T(8,128)S(1)}, f32[8,16,256]{2,1,0:T(8,128)}, u32[]{:S(2)}) copy-start(f32[8,16,256]{2,1,0:T(8,128)} %param.9) | copy-start | bytes 393220
  158.2 6.7 %copy-start.2 = (f32[8,16,256]{2,1,0:T(8,128)S(1)}, f32[8,16,256]{2,1,0:T(8,128)}, u32[]{:S(2)}) copy-start(f32[8,16,256]{2,1,0:T(8,128)} %param.10) | copy-start | bytes 393220
  158.4 8.6 %collective-permute-start = (f32[5,8,3,256]{3,0,2,1:T(8,128)S(1)}, f32[5,8,3,256]{3,0,2,1:T(8,128)S(1)}, u32[]{:S(2)}, u32[]{:S(2)}) collective-permute-start(f32[5,8,3,256]{3,0,2,1:T(8,128)S(1)} %get-tuple-element.342), channel_id=1, source_target_pairs={{2,0},{3,1},{6,4},{7,5},{10,8},{11,9},{14,12},{15,13},{18,16},{19,... | collective-permute-start | bytes 368648 | tf_op jit(solution)/shard_map/ppermute | solution.py:36
  159.7 7.7 %collective-permute-start.1 = (f32[5,8,3,256]{3,0,2,1:T(8,128)S(1)}, f32[5,8,3,256]{3,0,2,1:T(8,128)S(1)}, u32[]{:S(2)}, u32[]{:S(2)}) collective-permute-start(f32[5,8,3,256]{3,0,2,1:T(8,128)S(1)} %get-tuple-element.343), channel_id=1, source_target_pairs={{0,2},{1,3},{4,6},{5,7},{8,10},{9,11},{12,14},{13,15},{16,18},{17,... | collective-permute-start | bytes 368648 | tf_op jit(solution)/shard_map/ppermute | solution.py:33
  164.3 2.0 %collective-permute-start.2 = (f32[5,8,16,3]{3,0,2,1:T(8,128)S(1)}, f32[5,8,16,3]{3,0,2,1:T(8,128)S(1)}, u32[]{:S(2)}, u32[]{:S(2)}) collective-permute-start(f32[5,8,16,3]{3,0,2,1:T(8,128)S(1)} %get-tuple-element.340), channel_id=1, source_target_pairs={{1,0},{0,1},{3,2},{2,3},{5,4},{4,5},{7,6},{6,7},{9,8},{8,9},{11,10... | collective-permute-start | bytes 23048 | tf_op jit(solution)/shard_map/ppermute | solution.py:36
  164.4 2.6 %collective-permute-start.3 = (f32[5,8,16,3]{3,0,2,1:T(8,128)S(1)}, f32[5,8,16,3]{3,0,2,1:T(8,128)S(1)}, u32[]{:S(2)}, u32[]{:S(2)}) collective-permute-start(f32[5,8,16,3]{3,0,2,1:T(8,128)S(1)} %get-tuple-element.341), channel_id=1, source_target_pairs={{0,1},{1,0},{2,3},{3,2},{4,5},{5,4},{6,7},{7,6},{8,9},{9,8},{10,11... | collective-permute-start | bytes 23048 | tf_op jit(solution)/shard_map/ppermute | solution.py:33
Sparse Core Ops, SparseCore 0:
  10.7 72.3 all-reduce.3
  86.8 69.0 all-reduce.5
where the time goes:
time: 180 us
  blocking collectives  87 us (48%)
  waiting for transfers between devices  30.7 us (17%)
  other arithmetic  15.1 us (8%)
  between operations  13.7 us (8%)
  local copies, waits for them, and re-layouts  13 us (7%)
  loops' own time  9.38 us (5%)
  starting transfers between devices  6.47 us (4%)
  matrix products  4.26 us (2%)
    all_gather x2, blocking collectives, entering(): pieces = jax.tree.map(lambda part: lax.all_gather(part, axis), value)  63.9 us
    psum x1, waiting for transfers between devices, backward_sweep(): wrapped = lax.psum(weight * first_row, 'gx')  23.9 us
    unnamed x1, blocking collectives  23.1 us
    another operation x2, loops' own time, entering(): return lax.fori_loop(0, count - 1, lap, running)  9.38 us
    select_n x14, other arithmetic, lap(): jnp.where(position < mine, new, old)  9.17 us
    dynamic_slice x14, local copies, waits for them, and re-layouts, lap(): longer = join(running, jax.tree.map(lambda part: part[position], pieces))  8.77 us
    ppermute x2, starting transfers between devices, padded_2(): lax.ppermute(lax.slice_in_dim(block, block.shape[dim] - width, None, axis...  5.06 us
    psum x1, waiting for transfers between devices, forward_sweep(): wrapped = lax.psum(weight * last_row, 'gx')  4.41 us
  transfers between devices with their start and end apart: 6, of which 5 were waited for; matrix products, arithmetic and copies ran while one was open for 11% of the time, Pallas kernels for 0%

commit v1 on v0

v1 whole, which is shorter than its diff:
```python
import functools
import math

import jax
import jax.numpy as jnp
from jax import lax
from jax.experimental import pallas as pl
from jax.experimental.pallas import tpu as pltpu
from jax.sharding import PartitionSpec as P

MESH = pl.DeviceIdType.MESH
PIECES = 8
HALO = 8


def line_constants(total_cells):
    stiffness = total_cells * total_cells / 4.0
    half = 1.0 + 0.5 / stiffness
    decay = half - math.sqrt(half**2 - 1.0)
    return decay, decay / (stiffness * (1.0 - decay * decay))


def remote(src, dst, send_sem, recv_sem, target):
    return pltpu.make_async_remote_copy(
        src_ref=src, dst_ref=dst, send_sem=send_sem, recv_sem=recv_sem,
        device_id=target, device_id_type=MESH,
    )


def edges(block):
    width = block.shape[-1] // 2
    lane = lax.broadcasted_iota(jnp.int32, block.shape[:-1] + (width,), block.ndim - 1)
    return jnp.where(lane < width // 2, block[..., :width], block[..., width:])


def exchange_kernel(
    count_x, count_y, decay,
    a_ref, pq, pq_low, pq_high, pq_z, a_low, a_high, a_z,
    a_v, ends, own_in, own_out, pq_edges, a_edges,
    load_sem, send1, recv1, send2, recv2, send_a, recv_a, send_p, recv_p,
):
    fields, length, rows, lanes = a_v.shape
    stride = count_x // PIECES
    my_x, my_y, my_z = (lax.axis_index(name) for name in ("gx", "gy", "gz"))
    has_low, has_high = my_y > 0, my_y < count_y - 1
    low, high, other = {"gy": my_y - 1}, {"gy": my_y + 1}, {"gz": 1 - my_z}

    load = pltpu.make_async_copy(a_ref, a_v, load_sem)
    load.start()

    barrier = pltpu.get_barrier_semaphore()
    for step in range(1, count_x):
        peer = lax.rem(my_x + step, count_x)
        pl.semaphore_signal(barrier, inc=1, device_id={"gx": peer}, device_id_type=MESH)
    pl.semaphore_signal(barrier, inc=1, device_id=other, device_id_type=MESH)

    @pl.when(has_low)
    def _():
        pl.semaphore_signal(barrier, inc=1, device_id=low, device_id_type=MESH)

    @pl.when(has_high)
    def _():
        pl.semaphore_signal(barrier, inc=1, device_id=high, device_id_type=MESH)

    load.wait()
    upward = a_v[:, 0]
    downward = a_v[:, length - 1]
    for i in range(1, length):
        upward = a_v[:, i] + decay * upward
        downward = a_v[:, length - 1 - i] + decay * downward
    for yh in range(2):
        for kind in range(2):
            for zh in range(2):
                value = (upward, downward)[kind]
                ends[yh * 4 + kind * 2 + zh] = value[
                    :, yh * 8 : yh * 8 + 8, zh * (lanes // 2) : (zh + 1) * (lanes // 2)
                ]

    neighbours = has_low.astype(jnp.int32) + has_high.astype(jnp.int32)
    pl.semaphore_wait(barrier, count_x + neighbours)

    my_piece = my_x // stride
    owner = lax.rem(my_x, stride) == 0

    def end_copy(step):
        piece = lax.rem(my_piece + step, PIECES)
        target = piece * stride
        return target, remote(
            ends.at[piece], own_in.at[my_x], send1.at[step], recv1.at[my_x], {"gx": target}
        )

    for step in range(PIECES):
        if step == 0 and stride == 1:
            own_in[my_x] = ends[my_piece]
            continue
        target, copy = end_copy(step)

        @pl.when(target != my_x)
        def _():
            copy.start()

        if step == 0:

            @pl.when(target == my_x)
            def _():
                own_in[my_x] = ends[my_piece]

    a_edges[...] = edges(a_v[...])
    copy_az = remote(a_edges, a_z, send_a.at[0], recv_a.at[0], other)
    copy_az.start()
    copy_alow = remote(a_v.at[:, :, 0:HALO, :], a_high, send_a.at[1], recv_a.at[1], low)
    copy_ahigh = remote(
        a_v.at[:, :, rows - HALO : rows, :], a_low, send_a.at[2], recv_a.at[2], high
    )

    @pl.when(has_low)
    def _():
        copy_alow.start()

    @pl.when(has_high)
    def _():
        copy_ahigh.start()

    kind = lax.rem(my_piece // 2, 2)

    def result_copy(position, device):
        return remote(
            own_out.at[device], pq.at[my_piece], send2.at[device], recv2.at[my_piece],
            {"gx": device},
        )

    def own():
        for device in range(count_x):

            @pl.when(device != my_x)
            def _():
                remote(
                    own_in.at[device], own_in.at[device], send1.at[0], recv1.at[device],
                    {"gx": device},
                ).wait_recv()

        def index(position):
            return jnp.where(kind == 1, count_x - 1 - position, position)

        power = decay**length
        total = own_in[index(0)]
        for position in range(1, count_x):
            total = own_in[index(position)] + power * total
        total = total / (1.0 - power**count_x)
        for position in range(count_x):
            device = index(position)
            own_out[device] = total
            if position < count_x - 1:
                total = own_in[device] + power * total

            @pl.when(device != my_x)
            def _():
                result_copy(position, device).start()

            @pl.when(device == my_x)
            def _():
                pq[my_piece] = own_out[my_x]

    if stride == 1:
        own()
    else:
        pl.when(owner)(own)

    for piece in range(PIECES):

        @pl.when(piece * stride != my_x)
        def _():
            remote(
                own_out.at[0], pq.at[piece], send2.at[0], recv2.at[piece],
                {"gx": piece * stride},
            ).wait_recv()

    copy_plow = remote(pq.at[0:4], pq_high, send_p.at[1], recv_p.at[1], low)
    copy_phigh = remote(pq.at[4:8], pq_low, send_p.at[2], recv_p.at[2], high)

    @pl.when(has_low)
    def _():
        copy_plow.start()

    @pl.when(has_high)
    def _():
        copy_phigh.start()

    lane = lax.broadcasted_iota(jnp.int32, (fields, 8, lanes // 2), 2)
    for pair in range(4):
        pq_edges[pair] = jnp.where(lane < lanes // 4, pq[2 * pair], pq[2 * pair + 1])
    copy_pz = remote(pq_edges, pq_z, send_p.at[0], recv_p.at[0], other)
    copy_pz.start()

    copy_az.wait()
    copy_pz.wait()

    @pl.when(has_low)
    def _():
        copy_alow.wait_send()
        copy_plow.wait_send()
        copy_ahigh.wait_recv()
        copy_phigh.wait_recv()

    @pl.when(has_high)
    def _():
        copy_ahigh.wait_send()
        copy_phigh.wait_send()
        copy_alow.wait_recv()
        copy_plow.wait_recv()

    @pl.when(jnp.logical_not(has_low))
    def _():
        a_low[...] = jnp.zeros_like(a_low)
        pq_low[...] = jnp.zeros_like(pq_low)

    @pl.when(jnp.logical_not(has_high))
    def _():
        a_high[...] = jnp.zeros_like(a_high)
        pq_high[...] = jnp.zeros_like(pq_high)

    for step in range(PIECES):
        if step == 0 and stride == 1:
            continue
        target, copy = end_copy(step)

        @pl.when(target != my_x)
        def _():
            copy.wait_send()

    def finish():
        for device in range(count_x):

            @pl.when(device != my_x)
            def _():
                result_copy(0, device).wait_send()

    if stride == 1:
        finish()
    else:
        pl.when(owner)(finish)


def exchange(a, count_x, count_y, decay):
    fields, length, rows, lanes = a.shape
    half = lanes // 2
    shape = lambda *sizes: jax.ShapeDtypeStruct(sizes, jnp.float32)
    vmem = pl.BlockSpec(memory_space=pltpu.VMEM)
    dma = pltpu.SemaphoreType.DMA
    outs = [
        shape(PIECES, fields, 8, half), shape(4, fields, 8, half), shape(4, fields, 8, half),
        shape(4, fields, 8, half), shape(fields, length, HALO, lanes),
        shape(fields, length, HALO, lanes), shape(fields, length, rows, half),
    ]
    return pl.pallas_call(
        functools.partial(exchange_kernel, count_x, count_y, decay),
        out_shape=outs,
        in_specs=[pl.BlockSpec(memory_space=pl.ANY)],
        out_specs=[vmem] * len(outs),
        scratch_shapes=[
            pltpu.VMEM((fields, length, rows, lanes), jnp.float32),
            pltpu.VMEM((PIECES, fields, 8, half), jnp.float32),
            pltpu.VMEM((count_x, fields, 8, half), jnp.float32),
            pltpu.VMEM((count_x, fields, 8, half), jnp.float32),
            pltpu.VMEM((4, fields, 8, half), jnp.float32),
            pltpu.VMEM((fields, length, rows, half), jnp.float32),
            dma, dma((PIECES,)), dma((count_x,)), dma((count_x,)), dma((PIECES,)),
            dma((3,)), dma((3,)), dma((3,)), dma((3,)),
        ],
        compiler_params=pltpu.CompilerParams(
            collective_id=0, has_side_effects=True, vmem_limit_bytes=24 * 2**20
        ),
    )(a)


def pressure_wave_celerity(mass, level):
    attraction = 1.5 * (1.0 + 0.392 * (1.0 - jnp.sqrt(level))) ** 2
    q = 1.0 + 0.5 * mass - 0.0625 * mass * mass
    return level / (1.0 - 0.25 * mass) ** 2 - attraction * (
        2.0 * mass * q - mass * mass * (0.5 - 0.125 * mass)
    ) / (q * q)


def solved(block, up, down, decay, scale):
    length = len(block)
    upward, downward = [None] * length, [None] * length
    for i in range(length):
        up = block[i] + decay * up
        upward[i] = up
    for i in range(length - 1, -1, -1):
        down = decay * down
        downward[i] = down
        down = block[i] + down
    return [scale * (upward[i] + downward[i]) for i in range(length)]


def finish_kernel(
    decay, scale,
    m_ref, a, mass, level, pq, pq_low, pq_high, pq_z, a_low, a_high, a_z, out, ext, edge,
):
    fields, length, rows, lanes = a.shape

    def pair(ref, piece, f):
        return jnp.concatenate([ref[piece, f], ref[piece + 1, f]], axis=1)

    for f in range(fields):
        for block, values, at in (
            (a_low, (pair(pq_low, 0, f), pair(pq_low, 2, f)), 0),
            (a, (pair(pq, 0, f), pair(pq, 2, f)), HALO),
            (a, (pair(pq, 4, f), pair(pq, 6, f)), HALO + 8),
            (a_high, (pair(pq_high, 0, f), pair(pq_high, 2, f)), HALO + rows),
        ):
            start = at - HALO if block is a else 0
            cells = [block[f, i, start : start + 8, :] for i in range(length)]
            for i, value in enumerate(solved(cells, *values, decay, scale)):
                ext[f, i, at : at + 8, :] = value
        for yh in range(2):
            cells = [a_z[f, i, yh * 8 : yh * 8 + 8, :] for i in range(length)]
            values = (pq_z[yh * 2, f], pq_z[yh * 2 + 1, f])
            for i, value in enumerate(solved(cells, *values, decay, scale)):
                edge[f, i, yh * 8 : yh * 8 + 8, :] = value

    def plane(i, carry):
        celerity = pressure_wave_celerity(mass[i], level[i])
        slopes, centres = [], []
        for f in range(fields):
            at = lambda o: ext[f, i, HALO + o : HALO + o + rows, :]
            centre = at(0)
            ring = jnp.concatenate([centre, edge[f, i]], axis=1)
            turn = lambda o: pltpu.roll(ring, (-o) % ring.shape[1], 1)[:, :lanes]
            slopes.append(
                0.75 * ((at(1) - at(-1)) + (turn(1) - turn(-1)))
                - 0.15 * ((at(2) - at(-2)) + (turn(2) - turn(-2)))
                + ((at(3) - at(-3)) + (turn(3) - turn(-3))) * (1.0 / 60.0)
            )
            centres.append(centre)
        for j in range(fields):
            coupled = m_ref[0, j] * slopes[0]
            for k in range(1, fields):
                coupled = coupled + m_ref[k, j] * slopes[k]
            out[j, i] = centres[j] + celerity * coupled
        return carry

    lax.fori_loop(0, length, plane, 0)


def finish(m, a, mass, level, arrived, decay, scale):
    fields, length, rows, lanes = a.shape
    vmem = pl.BlockSpec(memory_space=pltpu.VMEM)
    return pl.pallas_call(
        functools.partial(finish_kernel, decay, scale),
        out_shape=jax.ShapeDtypeStruct(a.shape, jnp.float32),
        in_specs=[pl.BlockSpec(memory_space=pltpu.SMEM)] + [vmem] * (3 + len(arrived)),
        out_specs=vmem,
        scratch_shapes=[
            pltpu.VMEM((fields, length, rows + 2 * HALO, lanes), jnp.float32),
            pltpu.VMEM((fields, length, rows, lanes // 2), jnp.float32),
        ],
        compiler_params=pltpu.CompilerParams(vmem_limit_bytes=24 * 2**20),
    )(m, a, mass, level, *arrived)


def solution(mesh):
    count_x, count_y = mesh.shape["gx"], mesh.shape["gy"]

    def per_device(a, mass, level, m):
        decay, scale = line_constants(a.shape[1] * count_x)
        arrived = exchange(a, count_x, count_y, decay)
        return finish(m, a, mass, level, arrived, decay, scale)

    in_specs = (P(None, "gx", "gy", "gz"), P("gx", "gy", "gz"), P("gx", "gy", "gz"), P())
    out_specs = P(None, "gx", "gy", "gz")
    return jax.shard_map(
        per_device, mesh=mesh, in_specs=in_specs, out_specs=out_specs, check_vma=False
    )
```

time: 180 us -> 27.7 us (0.15)
  blocking collectives: 87 us -> 0 us
  waiting for transfers between devices: 30.7 us -> 0 us
  Pallas kernels: 0 us -> 25.7 us
  other arithmetic: 15.1 us -> 0 us
  between operations: 13.7 us -> 0.04 us
  local copies, waits for them, and re-layouts: 13 us -> 1.76 us
  loops' own time: 9.38 us -> 0 us
  starting transfers between devices: 6.47 us -> 0 us
  matrix products: 4.26 us -> 0 us
    all_gather x2 -> x0, blocking collectives: 63.9 us -> none  [entering(): pieces = jax.tree.map(lambda part: lax.all_gather(part, axis), value)]
    psum x2 -> x0, waiting for transfers between devices: 28.3 us -> none  [the longest x1 23.9 us: backward_sweep(): wrapped = lax.psum(weight * first_row, 'gx')]
    pallas_call x0 -> x2, Pallas kernels: none -> 25.7 us  [the longest x1 21.7 us: exchange(): pl.pallas_call(functools.partial(exchange_kernel, count_x, count_y, decay...]
    unnamed x1 -> x0, blocking collectives: 23.1 us -> none
    another operation x2 -> x0, loops' own time: 9.38 us -> none  [entering(): return lax.fori_loop(0, count - 1, lap, running)]
    select_n x14 -> x0, other arithmetic: 9.17 us -> none  [lap(): jnp.where(position < mine, new, old)]
    dynamic_slice x14 -> x0, local copies, waits for them, and re-layouts: 8.77 us -> none  [lap(): longer = join(running, jax.tree.map(lambda part: part[position], pieces))]
    ppermute x4 -> x0, starting transfers between devices: 6.42 us -> none  [the longest x2 5.06 us: padded_2(): lax.ppermute(lax.slice_in_dim(block, block.shape[dim] - width, None, axis...]
  transfers between devices with their start and end apart: 6 -> 0, of which waited for: 5 -> 0; matrix products, arithmetic and copies ran while one was open for 11% -> 0% of each run, Pallas kernels for 0% -> 0%
where the time goes in v1:
time: 27.7 us; the launch traced here: 27.5 us
  Pallas kernels  25.7 us (93%)
  local copies, waits for them, and re-layouts  1.76 us (6%)
    pallas_call x1, Pallas kernels, exchange(): pl.pallas_call(functools.partial(exchange_kernel, count_x, count_y, decay...  21.7 us
    pallas_call x1, Pallas kernels, finish(): pl.pallas_call(functools.partial(finish_kernel, decay, scale), out_shape=...  4.08 us
    unnamed x8, local copies, waits for them, and re-layouts  1.76 us

profile of v1, /device:TPU:0, one launch (start us, length us, event | category | flops | bytes accessed | tf_op | source)
XLA Modules:
  0.0 27.5 jit_solution(11883223496581829107)
XLA Ops:
  0.0 0.0 copy-start
  0.0 1.1 %copy-done = f32[5,8,16,256]{3,2,1,0:T(8,128)S(1)} copy-done((f32[5,8,16,256]{3,2,1,0:T(8,128)S(1)}, f32[5,8,16,256]{3,2,1,0:T(8,128)}, u32[]{:S(2)}) %copy-start) | copy-done | bytes 655384
  1.1 0.0 copy-start.1
  1.1 0.0 copy-start.2
  1.1 21.7 %shard_map.46 = (f32[8,5,8,128]{3,2,1,0:T(8,128)S(1)}, f32[4,5,8,128]{3,2,1,0:T(8,128)S(1)}, f32[4,5,8,128]{3,2,1,0:T(8,128)S(1)}, f32[4,5,8,128]{3,2,1,0:T(8,12...) custom-call(f32[5,8,16,256]{3,2,1,0:T(8,128)S(1)} %copy-done), custom_call_target="tpu_custom_call" | custom-call | tf_op jit(solution)/shard_map/pallas_call | solution.py:255
  22.8 0.0 copy-start.3
  22.8 0.0 copy-done.1
  22.8 0.0 copy-done.2
  22.8 0.7 %copy-done.3 = f32[5,5]{1,0:T(8,128)S(1)} copy-done((f32[5,5]{1,0:T(8,128)S(1)}, f32[5,5]{1,0:T(8,128)}, u32[]{:S(2)}) %copy-start.3) | copy-done | bytes 124
  23.4 4.1 %shard_map.47 = f32[5,8,16,256]{3,2,1,0:T(8,128)} custom-call(f32[5,5]{1,0:T(8,128)S(1)} %copy-done.3, f32[5,8,16,256]{3,2,1,0:T(8,128)S(1)} %copy-done, f32[8,16,256]{2,1,0:T(8,128)S(1)} %copy-done.1, f32[8,16,256]{2,1,0:T(8,128)S(1)} %copy-done.2, f32[8,5,8,128]{3,2,1,0:T(8,128)S(1)} %get-tuple-element.12.pq, ...), custom_call_target="tpu_custom_call" | custom-call | tf_op jit(solution)/shard_map/pallas_call | solution.py:350
Async XLA Ops:
  0.0 1.1 %copy-start = (f32[5,8,16,256]{3,2,1,0:T(8,128)S(1)}, f32[5,8,16,256]{3,2,1,0:T(8,128)}, u32[]{:S(2)}) copy-start(f32[5,8,16,256]{3,2,1,0:T(8,128)} %a.1) | copy-start | bytes 1966084
  1.1 21.7 %copy-start.1 = (f32[8,16,256]{2,1,0:T(8,128)S(1)}, f32[8,16,256]{2,1,0:T(8,128)}, u32[]{:S(2)}) copy-start(f32[8,16,256]{2,1,0:T(8,128)} %mass.1) | copy-start | bytes 393220
  1.1 21.7 %copy-start.2 = (f32[8,16,256]{2,1,0:T(8,128)S(1)}, f32[8,16,256]{2,1,0:T(8,128)}, u32[]{:S(2)}) copy-start(f32[8,16,256]{2,1,0:T(8,128)} %level.1) | copy-start | bytes 393220
  22.8 0.7 %copy-start.3 = (f32[5,5]{1,0:T(8,128)S(1)}, f32[5,5]{1,0:T(8,128)}, u32[]{:S(2)}) copy-start(f32[5,5]{1,0:T(8,128)} %m_ref.1) | copy-start | bytes 304

commit v2 on v1

v2 whole, which is shorter than its diff:
```python
import functools
import math

import jax
import jax.numpy as jnp
from jax import lax
from jax.experimental import pallas as pl
from jax.experimental.pallas import tpu as pltpu
from jax.sharding import PartitionSpec as P

MESH = pl.DeviceIdType.MESH
PIECES = 8
HALO = 8
STEPS = (4, 3, 5, 2, 6, 1, 7)


def line_constants(total_cells):
    stiffness = total_cells * total_cells / 4.0
    half = 1.0 + 0.5 / stiffness
    decay = half - math.sqrt(half**2 - 1.0)
    return decay, decay / (stiffness * (1.0 - decay * decay))


def remote(src, dst, send_sem, recv_sem, target):
    return pltpu.make_async_remote_copy(
        src_ref=src, dst_ref=dst, send_sem=send_sem, recv_sem=recv_sem,
        device_id=target, device_id_type=MESH,
    )


def edges(first, second):
    lane = lax.broadcasted_iota(jnp.int32, first.shape, first.ndim - 1)
    return jnp.where(lane < first.shape[-1] // 2, first, second)


def packed(first, second, low):
    row = lax.broadcasted_iota(jnp.int32, first.shape, first.ndim - 2)
    return jnp.where((row < 4) == low, first, pltpu.roll(second, 4, first.ndim - 2))


def slope(ext, edge, at_index, rows, lanes):
    at = lambda o: ext[(*at_index, slice(HALO + o, HALO + o + rows), slice(None))]
    ring = jnp.concatenate([at(0), edge[at_index]], axis=1)
    turn = lambda o: pltpu.roll(ring, (-o) % ring.shape[1], 1)[:, :lanes]
    return (
        0.75 * ((at(1) - at(-1)) + (turn(1) - turn(-1)))
        - 0.15 * ((at(2) - at(-2)) + (turn(2) - turn(-2)))
        + ((at(3) - at(-3)) + (turn(3) - turn(-3))) * (1.0 / 60.0)
    )


def exchange_kernel(
    count_x, count_y, decay, scale,
    a_ref, mass_ref, level_ref, m_ref, base, celerity, entering,
    a_v, mass, level, m, ends, own_in, own_out, pq, ext, u_edges, u_z, u_to_low, u_to_high,
    u_low, u_high, pq_ext, pq_edges, pq_z, p_to_low, p_to_high, p_low, p_high,
    load_sem, send1, recv1, send2, recv2, send_u, recv_u, send_p, recv_p,
):
    fields, length, rows, lanes = a_v.shape
    half = lanes // 2
    stride = count_x // PIECES
    my_x, my_y, my_z = (lax.axis_index(name) for name in ("gx", "gy", "gz"))
    has_low, has_high = my_y > 0, my_y < count_y - 1
    low, high, other = {"gy": my_y - 1}, {"gy": my_y + 1}, {"gz": 1 - my_z}

    load = pltpu.make_async_copy(a_ref, a_v, load_sem.at[0])
    load.start()
    later = [
        pltpu.make_async_copy(source, target, load_sem.at[1 + k])
        for k, (source, target) in enumerate(
            ((mass_ref, mass), (level_ref, level), (m_ref, m))
        )
    ]

    barrier = pltpu.get_barrier_semaphore()
    for step in range(1, count_x):
        peer = lax.rem(my_x + step, count_x)
        pl.semaphore_signal(barrier, inc=1, device_id={"gx": peer}, device_id_type=MESH)
    pl.semaphore_signal(barrier, inc=1, device_id=other, device_id_type=MESH)

    @pl.when(has_low)
    def _():
        pl.semaphore_signal(barrier, inc=1, device_id=low, device_id_type=MESH)

    @pl.when(has_high)
    def _():
        pl.semaphore_signal(barrier, inc=1, device_id=high, device_id_type=MESH)

    for copy in later:
        copy.start()

    load.wait()

    def field_ends(f, carry):
        upward = a_v[f, 0]
        downward = a_v[f, length - 1]
        for i in range(1, length):
            upward = a_v[f, i] + decay * upward
            downward = a_v[f, length - 1 - i] + decay * downward
        for yh in range(2):
            for kind in range(2):
                value = scale * (upward, downward)[kind][yh * 8 : yh * 8 + 8, :]
                for zh in range(2):
                    ends[yh * 4 + kind * 2 + zh, f] = value[:, zh * half : (zh + 1) * half]
        return carry

    lax.fori_loop(0, fields, field_ends, 0)

    neighbours = has_low.astype(jnp.int32) + has_high.astype(jnp.int32)
    pl.semaphore_wait(barrier, count_x + neighbours)

    my_piece = my_x // stride
    owner = lax.rem(my_x, stride) == 0
    steps = STEPS if stride == 1 else STEPS + (0,)

    def end_copy(step):
        piece = lax.rem(my_piece + step, PIECES)
        target = piece * stride
        return target, remote(
            ends.at[piece], own_in.at[my_x], send1.at[step], recv1.at[my_x], {"gx": target}
        )

    for step in steps:
        target, copy = end_copy(step)
        if stride == 1:
            copy.start()
        else:
            pl.when(target != my_x)(copy.start)
    if stride == 1:
        own_in[my_x] = ends[my_piece]
    else:

        @pl.when(owner)
        def _():
            own_in[my_x] = ends[my_piece]

    def field_solve(f, carry):
        upward = [a_v[f, 0]]
        for i in range(1, length):
            upward.append(a_v[f, i] + decay * upward[-1])
        down = jnp.zeros_like(upward[0])
        for i in range(length - 1, -1, -1):
            value = scale * (upward[i] + decay * down)
            down = a_v[f, i] + decay * down
            ext[f, i, HALO : HALO + rows, :] = value
            u_edges[f, i] = edges(value[:, :half], value[:, half:])
        for t in range(length // 2):
            u_to_low[f, t] = packed(
                ext[f, 2 * t, HALO : HALO + 8, :], ext[f, 2 * t + 1, HALO : HALO + 8, :], True
            )
            u_to_high[f, t] = packed(
                ext[f, 2 * t, HALO + rows - 8 : HALO + rows, :],
                ext[f, 2 * t + 1, HALO + rows - 8 : HALO + rows, :],
                False,
            )
        return carry

    lax.fori_loop(0, fields, field_solve, 0)
    copy_uz = remote(u_edges, u_z, send_u.at[0], recv_u.at[0], other)
    copy_uz.start()
    copy_ulow = remote(u_to_low, u_high, send_u.at[1], recv_u.at[1], low)
    copy_uhigh = remote(u_to_high, u_low, send_u.at[2], recv_u.at[2], high)
    pl.when(has_low)(copy_ulow.start)
    pl.when(has_high)(copy_uhigh.start)

    @pl.when(jnp.logical_not(has_low))
    def _():
        u_low[...] = jnp.zeros_like(u_low)
        p_low[...] = jnp.zeros_like(p_low)

    @pl.when(jnp.logical_not(has_high))
    def _():
        u_high[...] = jnp.zeros_like(u_high)
        p_high[...] = jnp.zeros_like(p_high)

    kind = lax.rem(my_piece // 2, 2)

    def result_copy(step):
        device = lax.rem(my_x + step, count_x)
        return remote(
            own_out.at[device], pq.at[my_piece], send2.at[step], recv2.at[my_piece],
            {"gx": device},
        )

    def own():
        for step in range(1, count_x):
            device = lax.rem(my_x + step, count_x)
            remote(
                own_in.at[device], own_in.at[device], send1.at[0], recv1.at[device],
                {"gx": device},
            ).wait_recv()

        def index(position):
            return jnp.where(kind == 1, count_x - 1 - position, position)

        power = decay**length
        total = own_in[index(0)]
        for position in range(1, count_x):
            total = own_in[index(position)] + power * total
        total = total * (1.0 / (1.0 - power**count_x))
        for position in range(count_x):
            device = index(position)
            own_out[device] = total
            if position < count_x - 1:
                total = own_in[device] + power * total
        for step in far_first:
            result_copy(step).start()
        pq[my_piece] = own_out[my_x]

    far_first = sorted(range(1, count_x), key=lambda step: abs(2 * step - count_x))
    if stride == 1:
        own()
    else:
        pl.when(owner)(own)

    copy_uz.wait_recv()
    pl.when(has_low)(copy_uhigh.wait_recv)
    pl.when(has_high)(copy_ulow.wait_recv)
    for copy in later:
        copy.wait()

    def field_halos(f, carry):
        for t in range(length // 2):
            ext[f, 2 * t, :HALO, :] = u_low[f, t]
            ext[f, 2 * t + 1, :HALO, :] = pltpu.roll(u_low[f, t], 4, 0)
            ext[f, 2 * t, HALO + rows :, :] = u_high[f, t]
            ext[f, 2 * t + 1, HALO + rows :, :] = pltpu.roll(u_high[f, t], 4, 0)
        return carry

    lax.fori_loop(0, fields, field_halos, 0)

    def couple(slopes, j):
        coupled = m[0, j] * slopes[0]
        for k in range(1, fields):
            coupled = coupled + m[k, j] * slopes[k]
        return coupled

    def plane(i, carry):
        speed = pressure_wave_celerity(mass[i], level[i])
        celerity[i] = speed
        slopes = [slope(ext, u_z, (f, i), rows, lanes) for f in range(fields)]
        for j in range(fields):
            base[j, i] = ext[j, i, HALO : HALO + rows, :] + speed * couple(slopes, j)
        return carry

    lax.fori_loop(0, length, plane, 0)

    for piece in range(PIECES):
        arrived = remote(
            own_out.at[0], pq.at[piece], send2.at[0], recv2.at[piece], {"gx": piece * stride}
        )
        pl.when(piece * stride != my_x)(arrived.wait_recv)

    for zh in range(2):
        p_to_low[zh] = packed(pq[zh], pq[2 + zh], True)
        p_to_high[zh] = packed(pq[4 + zh], pq[6 + zh], False)
    copy_plow = remote(p_to_low, p_high, send_p.at[1], recv_p.at[1], low)
    copy_phigh = remote(p_to_high, p_low, send_p.at[2], recv_p.at[2], high)
    pl.when(has_low)(copy_plow.start)
    pl.when(has_high)(copy_phigh.start)
    for kd in range(2):
        for yh in range(2):
            piece = yh * 4 + kd * 2
            pq_edges[kd, :, yh * 8 : yh * 8 + 8, :] = edges(pq[piece], pq[piece + 1])
            for zh in range(2):
                pq_ext[
                    kd, :, HALO + yh * 8 : HALO + yh * 8 + 8, zh * half : (zh + 1) * half
                ] = pq[piece + zh]
    copy_pz = remote(pq_edges, pq_z, send_p.at[0], recv_p.at[0], other)
    copy_pz.start()
    entering[0:2] = pq_ext[:, :, HALO : HALO + rows, :]

    for step in steps:
        target, copy = end_copy(step)
        if stride == 1:
            copy.wait_send()
        else:
            pl.when(target != my_x)(copy.wait_send)
    copy_uz.wait_send()
    pl.when(has_low)(copy_ulow.wait_send)
    pl.when(has_high)(copy_uhigh.wait_send)

    def sent():
        for step in far_first:
            result_copy(step).wait_send()

    if stride == 1:
        sent()
    else:
        pl.when(owner)(sent)

    copy_pz.wait()
    pl.when(has_low)(copy_plow.wait_send)
    pl.when(has_high)(copy_phigh.wait_send)
    pl.when(has_low)(copy_phigh.wait_recv)
    pl.when(has_high)(copy_plow.wait_recv)

    for zh in range(2):
        columns = slice(zh * half, (zh + 1) * half)
        pq_ext[0, :, :HALO, columns] = p_low[zh]
        pq_ext[1, :, :HALO, columns] = pltpu.roll(p_low[zh], 4, 1)
        pq_ext[0, :, HALO + rows :, columns] = p_high[zh]
        pq_ext[1, :, HALO + rows :, columns] = pltpu.roll(p_high[zh], 4, 1)
    for kd in range(2):
        slopes = [slope(pq_ext, pq_z, (kd, f), rows, lanes) for f in range(fields)]
        for j in range(fields):
            entering[2 + kd, j] = couple(slopes, j)


def exchange(a, mass, level, m, count_x, count_y, decay, scale):
    fields, length, rows, lanes = a.shape
    half = lanes // 2
    vmem = pl.BlockSpec(memory_space=pltpu.VMEM)
    hbm = pl.BlockSpec(memory_space=pltpu.HBM)
    dma = pltpu.SemaphoreType.DMA
    buffer = lambda *sizes: pltpu.VMEM(sizes, jnp.float32)
    shape = lambda *sizes: jax.ShapeDtypeStruct(sizes, jnp.float32)
    return pl.pallas_call(
        functools.partial(exchange_kernel, count_x, count_y, decay, scale),
        out_shape=[
            shape(*a.shape), shape(length, rows, lanes), shape(4, fields, rows, lanes)
        ],
        in_specs=[hbm] * 4,
        out_specs=[vmem] * 3,
        scratch_shapes=[
            buffer(*a.shape), buffer(length, rows, lanes), buffer(length, rows, lanes),
            pltpu.SMEM((fields, fields), jnp.float32),
            buffer(PIECES, fields, 8, half),
            buffer(count_x, fields, 8, half),
            buffer(count_x, fields, 8, half),
            buffer(PIECES, fields, 8, half),
            buffer(fields, length, rows + 2 * HALO, lanes),
            buffer(fields, length, rows, half), buffer(fields, length, rows, half),
            buffer(fields, length // 2, 8, lanes), buffer(fields, length // 2, 8, lanes),
            buffer(fields, length // 2, 8, lanes), buffer(fields, length // 2, 8, lanes),
            buffer(2, fields, rows + 2 * HALO, lanes),
            buffer(2, fields, rows, half), buffer(2, fields, rows, half),
            buffer(2, fields, 8, half), buffer(2, fields, 8, half),
            buffer(2, fields, 8, half), buffer(2, fields, 8, half),
            dma((4,)), dma((PIECES,)), dma((count_x,)), dma((count_x,)), dma((PIECES,)),
            dma((3,)), dma((3,)), dma((3,)), dma((3,)),
        ],
        compiler_params=pltpu.CompilerParams(
            collective_id=0, has_side_effects=True, vmem_limit_bytes=24 * 2**20
        ),
    )(a, mass, level, m)


def pressure_wave_celerity(mass, level):
    attraction = 1.5 * (1.0 + 0.392 * (1.0 - jnp.sqrt(level))) ** 2
    q = 1.0 + 0.5 * mass - 0.0625 * mass * mass
    return level / (1.0 - 0.25 * mass) ** 2 - attraction * (
        2.0 * mass * q - mass * mass * (0.5 - 0.125 * mass)
    ) / (q * q)


def finish_kernel(decay, base, celerity, entering, out, result, sems):
    fields, length, rows, lanes = base.shape
    copies = []
    for i in range(length):
        up, down = decay ** (i + 1), decay ** (length - i)
        for j in range(fields):
            straight = up * entering[0, j] + down * entering[1, j]
            coupled = up * entering[2, j] + down * entering[3, j]
            result[j, i] = base[j, i] + straight + celerity[i] * coupled
        copies.append(pltpu.make_async_copy(result.at[:, i], out.at[:, i], sems.at[i]))
        copies[-1].start()
    for copy in copies:
        copy.wait()


def finish(base, celerity, entering, decay):
    vmem = pl.BlockSpec(memory_space=pltpu.VMEM)
    return pl.pallas_call(
        functools.partial(finish_kernel, decay),
        out_shape=jax.ShapeDtypeStruct(base.shape, jnp.float32),
        in_specs=[vmem] * 3,
        out_specs=pl.BlockSpec(memory_space=pltpu.HBM),
        scratch_shapes=[
            pltpu.VMEM(base.shape, jnp.float32), pltpu.SemaphoreType.DMA((base.shape[1],))
        ],
        compiler_params=pltpu.CompilerParams(vmem_limit_bytes=24 * 2**20),
    )(base, celerity, entering)


def solution(mesh):
    count_x, count_y = mesh.shape["gx"], mesh.shape["gy"]

    def per_device(a, mass, level, m):
        decay, scale = line_constants(a.shape[1] * count_x)
        parts = exchange(a, mass, level, m, count_x, count_y, decay, scale)
        return finish(*parts, decay)

    in_specs = (P(None, "gx", "gy", "gz"), P("gx", "gy", "gz"), P("gx", "gy", "gz"), P())
    out_specs = P(None, "gx", "gy", "gz")
    return jax.shard_map(
        per_device, mesh=mesh, in_specs=in_specs, out_specs=out_specs, check_vma=False
    )
```

time: 27.7 us -> 26.1 us (0.942)
  Pallas kernels: 25.7 us -> 22.3 us
  local copies, waits for them, and re-layouts: 1.76 us -> 3.58 us
    pallas_call x1, Pallas kernels: 4.08 us -> 0.93 us  [finish(): pl.pallas_call(functools.partial(finish_kernel, decay), out_shape=jax.Sha...]
    unnamed x8, local copies, waits for them, and re-layouts: 1.76 us -> 3.58 us
where the time goes in v2:
time: 26.1 us; the launch traced here: 25.9 us
  Pallas kernels  22.3 us (85%)
  local copies, waits for them, and re-layouts  3.58 us (14%)
    pallas_call x1, Pallas kernels, exchange(): pl.pallas_call(functools.partial(exchange_kernel, count_x, count_y, decay...  21.4 us
    unnamed x8, local copies, waits for them, and re-layouts  3.58 us
    pallas_call x1, Pallas kernels, finish(): pl.pallas_call(functools.partial(finish_kernel, decay), out_shape=jax.Sha...  0.93 us

profile of v2, /device:TPU:0, one launch (start us, length us, event | category | flops | bytes accessed | tf_op | source)
XLA Modules:
  0.0 25.9 jit_solution(10875826295730230387)
XLA Ops:
  0.0 0.0 copy-start
  0.0 1.1 %copy-done = f32[5,8,16,256]{3,2,1,0:T(8,128)S(1)} copy-done((f32[5,8,16,256]{3,2,1,0:T(8,128)S(1)}, f32[5,8,16,256]{3,2,1,0:T(8,128)}, u32[]{:S(2)}) %copy-start) | copy-done | bytes 655384
  1.1 0.0 copy-start.1
  1.1 0.9 %copy-done.1 = f32[8,16,256]{2,1,0:T(8,128)S(1)} copy-done((f32[8,16,256]{2,1,0:T(8,128)S(1)}, f32[8,16,256]{2,1,0:T(8,128)}, u32[]{:S(2)}) %copy-start.1) | copy-done | bytes 131096
  2.0 0.0 copy-start.2
  2.0 0.9 %copy-done.2 = f32[8,16,256]{2,1,0:T(8,128)S(1)} copy-done((f32[8,16,256]{2,1,0:T(8,128)S(1)}, f32[8,16,256]{2,1,0:T(8,128)}, u32[]{:S(2)}) %copy-start.2) | copy-done | bytes 131096
  2.9 0.0 copy-start.3
  2.9 0.7 %copy-done.3 = f32[5,5]{1,0:T(8,128)S(1)} copy-done((f32[5,5]{1,0:T(8,128)S(1)}, f32[5,5]{1,0:T(8,128)}, u32[]{:S(2)}) %copy-start.3) | copy-done | bytes 124
  3.6 21.4 %shard_map.46 = (f32[5,8,16,256]{3,2,1,0:T(8,128)S(1)}, f32[8,16,256]{2,1,0:T(8,128)S(1)}, f32[4,5,16,256]{3,2,1,0:T(8,128)S(1)}) custom-call(f32[5,8,16,256]{3,2,1,0:T(8,128)S(1)} %copy-done, f32[8,16,256]{2,1,0:T(8,128)S(1)} %copy-done.1, f32[8,16,256]{2,1,0:T(8,128)S(1)} %copy-done.2, f32[5,5]{1,0:T(8,128)S(1)} %copy-done.3), custom_call_target="tpu_custom_call" | custom-call | tf_op jit(solution)/shard_map/pallas_call | solution.py:318
  25.0 0.9 %shard_map.47 = f32[5,8,16,256]{3,2,1,0:T(8,128)} custom-call(f32[5,8,16,256]{3,2,1,0:T(8,128)S(1)} %get-tuple-element.8.base, f32[8,16,256]{2,1,0:T(8,128)S(1)} %get-tuple-element.9.celerity, f32[4,5,16,256]{3,2,1,0:T(8,128)S(1)} %get-tuple-element.10.entering), custom_call_target="tpu_custom_call" | custom-call | tf_op jit(solution)/shard_map/pallas_call | solution.py:374
Async XLA Ops:
  0.0 1.1 %copy-start = (f32[5,8,16,256]{3,2,1,0:T(8,128)S(1)}, f32[5,8,16,256]{3,2,1,0:T(8,128)}, u32[]{:S(2)}) copy-start(f32[5,8,16,256]{3,2,1,0:T(8,128)} %a_ref.1) | copy-start | bytes 1966084
  1.1 0.9 %copy-start.1 = (f32[8,16,256]{2,1,0:T(8,128)S(1)}, f32[8,16,256]{2,1,0:T(8,128)}, u32[]{:S(2)}) copy-start(f32[8,16,256]{2,1,0:T(8,128)} %mass_ref.1) | copy-start | bytes 393220
  2.0 0.9 %copy-start.2 = (f32[8,16,256]{2,1,0:T(8,128)S(1)}, f32[8,16,256]{2,1,0:T(8,128)}, u32[]{:S(2)}) copy-start(f32[8,16,256]{2,1,0:T(8,128)} %level_ref.1) | copy-start | bytes 393220
  2.9 0.7 %copy-start.3 = (f32[5,5]{1,0:T(8,128)S(1)}, f32[5,5]{1,0:T(8,128)}, u32[]{:S(2)}) copy-start(f32[5,5]{1,0:T(8,128)} %m_ref.1) | copy-start | bytes 304

commit v3 on v2

--- a/solution.py
+++ b/solution.py
@@ -343,7 +343,7 @@
         compiler_params=pltpu.CompilerParams(
             collective_id=0, has_side_effects=True, vmem_limit_bytes=24 * 2**20
         ),
-    )(a, mass, level, m)
+    )(*(pltpu.with_memory_space_constraint(x, pltpu.HBM) for x in (a, mass, level, m)))
 
 
 def pressure_wave_celerity(mass, level):

time: 26.1 us -> 22.3 us (0.85)
  local copies, waits for them, and re-layouts: 3.58 us -> 0 us
    unnamed x8 -> x0, local copies, waits for them, and re-layouts: 3.58 us -> none
where the time goes in v3:
time: 22.3 us; the launch traced here: 22.1 us
  Pallas kernels  22.1 us (99%)
    pallas_call x1, Pallas kernels, exchange(): pl.pallas_call(functools.partial(exchange_kernel, count_x, count_y, decay...  21.2 us
    pallas_call x1, Pallas kernels, finish(): pl.pallas_call(functools.partial(finish_kernel, decay), out_shape=jax.Sha...  0.93 us

profile of v3, /device:TPU:0, one launch (start us, length us, event | category | flops | bytes accessed | tf_op | source)
XLA Modules:
  0.0 22.1 jit_solution(6245189103777128120)
XLA Ops:
  0.0 21.2 %shard_map.46 = (f32[5,8,16,256]{3,2,1,0:T(8,128)S(1)}, f32[8,16,256]{2,1,0:T(8,128)S(1)}, f32[4,5,16,256]{3,2,1,0:T(8,128)S(1)}) custom-call(f32[5,8,16,256]{3,2,1,0:T(8,128)} %a_ref.1, f32[8,16,256]{2,1,0:T(8,128)} %mass_ref.1, f32[8,16,256]{2,1,0:T(8,128)} %level_ref.1, f32[5,5]{1,0:T(8,128)} %m_ref.1), custom_call_target="tpu_custom_call" | custom-call | tf_op jit(solution)/shard_map/pallas_call | solution.py:318
  21.2 0.9 %shard_map.47 = f32[5,8,16,256]{3,2,1,0:T(8,128)} custom-call(f32[5,8,16,256]{3,2,1,0:T(8,128)S(1)} %get-tuple-element.8.base, f32[8,16,256]{2,1,0:T(8,128)S(1)} %get-tuple-element.9.celerity, f32[4,5,16,256]{3,2,1,0:T(8,128)S(1)} %get-tuple-element.10.entering), custom_call_target="tpu_custom_call" | custom-call | tf_op jit(solution)/shard_map/pallas_call | solution.py:374

commit v4 on v3

--- a/solution.py
+++ b/solution.py
@@ -63,10 +63,15 @@
     has_low, has_high = my_y > 0, my_y < count_y - 1
     low, high, other = {"gy": my_y - 1}, {"gy": my_y + 1}, {"gz": 1 - my_z}
 
-    load = pltpu.make_async_copy(a_ref, a_v, load_sem.at[0])
-    load.start()
+    middle = (fields + 1) // 2
+    groups = tuple(enumerate((slice(0, middle), slice(middle, fields))))
+    loads = [
+        pltpu.make_async_copy(a_ref.at[part], a_v.at[part], load_sem.at[g]) for g, part in groups
+    ]
+    for copy in loads:
+        copy.start()
     later = [
-        pltpu.make_async_copy(source, target, load_sem.at[1 + k])
+        pltpu.make_async_copy(source, target, load_sem.at[2 + k])
         for k, (source, target) in enumerate(
             ((mass_ref, mass), (level_ref, level), (m_ref, m))
         )
@@ -88,8 +93,6 @@
 
     for copy in later:
         copy.start()
-
-    load.wait()
 
     def field_ends(f, carry):
         upward = a_v[f, 0]
@@ -104,28 +107,31 @@
                     ends[yh * 4 + kind * 2 + zh, f] = value[:, zh * half : (zh + 1) * half]
         return carry
 
-    lax.fori_loop(0, fields, field_ends, 0)
-
-    neighbours = has_low.astype(jnp.int32) + has_high.astype(jnp.int32)
-    pl.semaphore_wait(barrier, count_x + neighbours)
-
     my_piece = my_x // stride
     owner = lax.rem(my_x, stride) == 0
     steps = STEPS if stride == 1 else STEPS + (0,)
 
-    def end_copy(step):
+    def end_copy(group, step):
+        g, part = group
         piece = lax.rem(my_piece + step, PIECES)
         target = piece * stride
         return target, remote(
-            ends.at[piece], own_in.at[my_x], send1.at[step], recv1.at[my_x], {"gx": target}
-        )
-
-    for step in steps:
-        target, copy = end_copy(step)
-        if stride == 1:
-            copy.start()
-        else:
-            pl.when(target != my_x)(copy.start)
+            ends.at[piece, part], own_in.at[my_x, part], send1.at[g, step], recv1.at[g, my_x],
+            {"gx": target},
+        )
+
+    neighbours = has_low.astype(jnp.int32) + has_high.astype(jnp.int32)
+    for g, part in groups:
+        loads[g].wait()
+        lax.fori_loop(part.start, part.stop, field_ends, 0)
+        if g == 0:
+            pl.semaphore_wait(barrier, count_x + neighbours)
+        for step in steps:
+            target, copy = end_copy((g, part), step)
+            if stride == 1:
+                copy.start()
+            else:
+                pl.when(target != my_x)(copy.start)
     if stride == 1:
         own_in[my_x] = ends[my_piece]
     else:
@@ -175,43 +181,46 @@
 
     kind = lax.rem(my_piece // 2, 2)
 
-    def result_copy(step):
+    def result_copy(group, step):
+        g, part = group
         device = lax.rem(my_x + step, count_x)
         return remote(
-            own_out.at[device], pq.at[my_piece], send2.at[step], recv2.at[my_piece],
-            {"gx": device},
-        )
-
-    def own():
+            own_out.at[device, part], pq.at[my_piece, part], send2.at[g, step],
+            recv2.at[g, my_piece], {"gx": device},
+        )
+
+    def own(group):
+        g, part = group
         for step in range(1, count_x):
             device = lax.rem(my_x + step, count_x)
             remote(
-                own_in.at[device], own_in.at[device], send1.at[0], recv1.at[device],
-                {"gx": device},
+                own_in.at[device, part], own_in.at[device, part], send1.at[g, 0],
+                recv1.at[g, device], {"gx": device},
             ).wait_recv()
 
         def index(position):
             return jnp.where(kind == 1, count_x - 1 - position, position)
 
         power = decay**length
-        total = own_in[index(0)]
+        total = own_in[index(0), part]
         for position in range(1, count_x):
-            total = own_in[index(position)] + power * total
+            total = own_in[index(position), part] + power * total
         total = total * (1.0 / (1.0 - power**count_x))
         for position in range(count_x):
             device = index(position)
-            own_out[device] = total
+            own_out[device, part] = total
             if position < count_x - 1:
-                total = own_in[device] + power * total
+                total = own_in[device, part] + power * total
         for step in far_first:
-            result_copy(step).start()
-        pq[my_piece] = own_out[my_x]
+            result_copy(group, step).start()
+        pq[my_piece, part] = own_out[my_x, part]
 
     far_first = sorted(range(1, count_x), key=lambda step: abs(2 * step - count_x))
-    if stride == 1:
-        own()
-    else:
-        pl.when(owner)(own)
+    for group in groups:
+        if stride == 1:
+            own(group)
+        else:
+            pl.when(owner)(functools.partial(own, group))
 
     copy_uz.wait_recv()
     pl.when(has_low)(copy_uhigh.wait_recv)
@@ -243,57 +252,72 @@
             base[j, i] = ext[j, i, HALO : HALO + rows, :] + speed * couple(slopes, j)
         return carry
 
-    lax.fori_loop(0, length, plane, 0)
-
-    for piece in range(PIECES):
-        arrived = remote(
-            own_out.at[0], pq.at[piece], send2.at[0], recv2.at[piece], {"gx": piece * stride}
-        )
-        pl.when(piece * stride != my_x)(arrived.wait_recv)
-
-    for zh in range(2):
-        p_to_low[zh] = packed(pq[zh], pq[2 + zh], True)
-        p_to_high[zh] = packed(pq[4 + zh], pq[6 + zh], False)
-    copy_plow = remote(p_to_low, p_high, send_p.at[1], recv_p.at[1], low)
-    copy_phigh = remote(p_to_high, p_low, send_p.at[2], recv_p.at[2], high)
-    pl.when(has_low)(copy_plow.start)
-    pl.when(has_high)(copy_phigh.start)
+    last = []
+    for g, part in groups:
+        lax.fori_loop(g * length // 2, (g + 1) * length // 2, plane, 0)
+        for piece in range(PIECES):
+            arrived = remote(
+                own_out.at[0, part], pq.at[piece, part], send2.at[g, 0], recv2.at[g, piece],
+                {"gx": piece * stride},
+            )
+            pl.when(piece * stride != my_x)(arrived.wait_recv)
+        for zh in range(2):
+            p_to_low[zh, part] = packed(pq[zh, part], pq[2 + zh, part], True)
+            p_to_high[zh, part] = packed(pq[4 + zh, part], pq[6 + zh, part], False)
+        copy_plow = remote(
+            p_to_low.at[:, part], p_high.at[:, part], send_p.at[g, 1], recv_p.at[g, 1], low
+        )
+        copy_phigh = remote(
+            p_to_high.at[:, part], p_low.at[:, part], send_p.at[g, 2], recv_p.at[g, 2], high
+        )
+        pl.when(has_low)(copy_plow.start)
+        pl.when(has_high)(copy_phigh.start)
+        for kd in range(2):
+            for yh in range(2):
+                piece = yh * 4 + kd * 2
+                pq_edges[kd, part, yh * 8 : yh * 8 + 8, :] = edges(
+                    pq[piece, part], pq[piece + 1, part]
+                )
+        copy_pz = remote(
+            pq_edges.at[:, part], pq_z.at[:, part], send_p.at[g, 0], recv_p.at[g, 0], other
+        )
+        copy_pz.start()
+        last.append((copy_pz, copy_plow, copy_phigh))
     for kd in range(2):
         for yh in range(2):
-            piece = yh * 4 + kd * 2
-            pq_edges[kd, :, yh * 8 : yh * 8 + 8, :] = edges(pq[piece], pq[piece + 1])
             for zh in range(2):
                 pq_ext[
                     kd, :, HALO + yh * 8 : HALO + yh * 8 + 8, zh * half : (zh + 1) * half
-                ] = pq[piece + zh]
-    copy_pz = remote(pq_edges, pq_z, send_p.at[0], recv_p.at[0], other)
-    copy_pz.start()
+                ] = pq[yh * 4 + kd * 2 + zh]
     entering[0:2] = pq_ext[:, :, HALO : HALO + rows, :]
 
-    for step in steps:
-        target, copy = end_copy(step)
-        if stride == 1:
-            copy.wait_send()
-        else:
-            pl.when(target != my_x)(copy.wait_send)
+    for group in groups:
+        for step in steps:
+            target, copy = end_copy(group, step)
+            if stride == 1:
+                copy.wait_send()
+            else:
+                pl.when(target != my_x)(copy.wait_send)
     copy_uz.wait_send()
     pl.when(has_low)(copy_ulow.wait_send)
     pl.when(has_high)(copy_uhigh.wait_send)
 
     def sent():
-        for step in far_first:
-            result_copy(step).wait_send()
+        for group in groups:
+            for step in far_first:
+                result_copy(group, step).wait_send()
 
     if stride == 1:
         sent()
     else:
         pl.when(owner)(sent)
 
-    copy_pz.wait()
-    pl.when(has_low)(copy_plow.wait_send)
-    pl.when(has_high)(copy_phigh.wait_send)
-    pl.when(has_low)(copy_phigh.wait_recv)
-    pl.when(has_high)(copy_plow.wait_recv)
+    for copy_pz, copy_plow, copy_phigh in last:
+        copy_pz.wait()
+        pl.when(has_low)(copy_plow.wait_send)
+        pl.when(has_high)(copy_phigh.wait_send)
+        pl.when(has_low)(copy_phigh.wait_recv)
+        pl.when(has_high)(copy_plow.wait_recv)
 
     for zh in range(2):
         columns = slice(zh * half, (zh + 1) * half)
@@ -337,8 +361,8 @@
             buffer(2, fields, rows, half), buffer(2, fields, rows, half),
             buffer(2, fields, 8, half), buffer(2, fields, 8, half),
             buffer(2, fields, 8, half), buffer(2, fields, 8, half),
-            dma((4,)), dma((PIECES,)), dma((count_x,)), dma((count_x,)), dma((PIECES,)),
-            dma((3,)), dma((3,)), dma((3,)), dma((3,)),
+            dma((5,)), dma((2, PIECES)), dma((2, count_x)), dma((2, count_x)),
+            dma((2, PIECES)), dma((3,)), dma((3,)), dma((2, 3)), dma((2, 3)),
         ],
         compiler_params=pltpu.CompilerParams(
             collective_id=0, has_side_effects=True, vmem_limit_bytes=24 * 2**20

time: 22.3 us -> 22.4 us (level)
  no operation moved by 1% of the time
where the time goes in v4:
time: 22.4 us; the launch traced here: 22.3 us
  Pallas kernels  22.3 us (100%)
    pallas_call x1, Pallas kernels, exchange(): pl.pallas_call(functools.partial(exchange_kernel, count_x, count_y, decay...  21.4 us
    pallas_call x1, Pallas kernels, finish(): pl.pallas_call(functools.partial(finish_kernel, decay), out_shape=jax.Sha...  0.93 us

profile of v4, /device:TPU:0, one launch (start us, length us, event | category | flops | bytes accessed | tf_op | source)
XLA Modules:
  0.0 22.3 jit_solution(14131816704542056887)
XLA Ops:
  0.0 21.4 %shard_map.46 = (f32[5,8,16,256]{3,2,1,0:T(8,128)S(1)}, f32[8,16,256]{2,1,0:T(8,128)S(1)}, f32[4,5,16,256]{3,2,1,0:T(8,128)S(1)}) custom-call(f32[5,8,16,256]{3,2,1,0:T(8,128)} %a_ref.1, f32[8,16,256]{2,1,0:T(8,128)} %mass_ref.1, f32[8,16,256]{2,1,0:T(8,128)} %level_ref.1, f32[5,5]{1,0:T(8,128)} %m_ref.1), custom_call_target="tpu_custom_call" | custom-call | tf_op jit(solution)/shard_map/pallas_call | solution.py:342
  21.4 0.9 %shard_map.47 = f32[5,8,16,256]{3,2,1,0:T(8,128)} custom-call(f32[5,8,16,256]{3,2,1,0:T(8,128)S(1)} %get-tuple-element.8.base, f32[8,16,256]{2,1,0:T(8,128)S(1)} %get-tuple-element.9.celerity, f32[4,5,16,256]{3,2,1,0:T(8,128)S(1)} %get-tuple-element.10.entering), custom_call_target="tpu_custom_call" | custom-call | tf_op jit(solution)/shard_map/pallas_call | solution.py:398

commit v5 on v3

--- a/solution.py
+++ b/solution.py
@@ -53,7 +53,7 @@
     count_x, count_y, decay, scale,
     a_ref, mass_ref, level_ref, m_ref, base, celerity, entering,
     a_v, mass, level, m, ends, own_in, own_out, pq, ext, u_edges, u_z, u_to_low, u_to_high,
-    u_low, u_high, pq_ext, pq_edges, pq_z, p_to_low, p_to_high, p_low, p_high,
+    u_low, u_high, pq_ext, pq_edges, pq_z, p_low, p_high,
     load_sem, send1, recv1, send2, recv2, send_u, recv_u, send_p, recv_p,
 ):
     fields, length, rows, lanes = a_v.shape
@@ -80,11 +80,17 @@
 
     @pl.when(has_low)
     def _():
-        pl.semaphore_signal(barrier, inc=1, device_id=low, device_id_type=MESH)
+        for x in range(count_x):
+            pl.semaphore_signal(
+                barrier, inc=1, device_id={"gx": x, "gy": my_y - 1}, device_id_type=MESH
+            )
 
     @pl.when(has_high)
     def _():
-        pl.semaphore_signal(barrier, inc=1, device_id=high, device_id_type=MESH)
+        for x in range(count_x):
+            pl.semaphore_signal(
+                barrier, inc=1, device_id={"gx": x, "gy": my_y + 1}, device_id_type=MESH
+            )
 
     for copy in later:
         copy.start()
@@ -107,7 +113,7 @@
     lax.fori_loop(0, fields, field_ends, 0)
 
     neighbours = has_low.astype(jnp.int32) + has_high.astype(jnp.int32)
-    pl.semaphore_wait(barrier, count_x + neighbours)
+    pl.semaphore_wait(barrier, count_x * (1 + neighbours))
 
     my_piece = my_x // stride
     owner = lax.rem(my_x, stride) == 0
@@ -182,6 +188,24 @@
             {"gx": device},
         )
 
+    slot = lax.rem(my_piece, 4)
+    to_low = jnp.logical_and(my_piece < 4, has_low)
+    to_high = jnp.logical_and(my_piece >= 4, has_high)
+
+    def low_copy(step):
+        device = lax.rem(my_x + step, count_x)
+        return remote(
+            own_out.at[device], p_high.at[slot], send_p.at[1 + step], recv_p.at[5 + slot],
+            {"gx": device, "gy": my_y - 1},
+        )
+
+    def high_copy(step):
+        device = lax.rem(my_x + step, count_x)
+        return remote(
+            own_out.at[device], p_low.at[slot], send_p.at[1 + step], recv_p.at[1 + slot],
+            {"gx": device, "gy": my_y + 1},
+        )
+
     def own():
         for step in range(1, count_x):
             device = lax.rem(my_x + step, count_x)
@@ -205,6 +229,17 @@
                 total = own_in[device] + power * total
         for step in far_first:
             result_copy(step).start()
+
+        @pl.when(to_low)
+        def _():
+            for step in far_first + [0]:
+                low_copy(step).start()
+
+        @pl.when(to_high)
+        def _():
+            for step in far_first + [0]:
+                high_copy(step).start()
+
         pq[my_piece] = own_out[my_x]
 
     far_first = sorted(range(1, count_x), key=lambda step: abs(2 * step - count_x))
@@ -251,13 +286,6 @@
         )
         pl.when(piece * stride != my_x)(arrived.wait_recv)
 
-    for zh in range(2):
-        p_to_low[zh] = packed(pq[zh], pq[2 + zh], True)
-        p_to_high[zh] = packed(pq[4 + zh], pq[6 + zh], False)
-    copy_plow = remote(p_to_low, p_high, send_p.at[1], recv_p.at[1], low)
-    copy_phigh = remote(p_to_high, p_low, send_p.at[2], recv_p.at[2], high)
-    pl.when(has_low)(copy_plow.start)
-    pl.when(has_high)(copy_phigh.start)
     for kd in range(2):
         for yh in range(2):
             piece = yh * 4 + kd * 2
@@ -284,23 +312,44 @@
         for step in far_first:
             result_copy(step).wait_send()
 
+        @pl.when(to_low)
+        def _():
+            for step in far_first + [0]:
+                low_copy(step).wait_send()
+
+        @pl.when(to_high)
+        def _():
+            for step in far_first + [0]:
+                high_copy(step).wait_send()
+
     if stride == 1:
         sent()
     else:
         pl.when(owner)(sent)
 
     copy_pz.wait()
-    pl.when(has_low)(copy_plow.wait_send)
-    pl.when(has_high)(copy_phigh.wait_send)
-    pl.when(has_low)(copy_phigh.wait_recv)
-    pl.when(has_high)(copy_plow.wait_recv)
+
+    @pl.when(has_low)
+    def _():
+        for k in range(4):
+            remote(
+                own_out.at[0], p_low.at[k], send_p.at[0], recv_p.at[1 + k],
+                {"gx": (4 + k) * stride, "gy": my_y - 1},
+            ).wait_recv()
+
+    @pl.when(has_high)
+    def _():
+        for k in range(4):
+            remote(
+                own_out.at[0], p_high.at[k], send_p.at[0], recv_p.at[5 + k],
+                {"gx": k * stride, "gy": my_y + 1},
+            ).wait_recv()
 
     for zh in range(2):
         columns = slice(zh * half, (zh + 1) * half)
-        pq_ext[0, :, :HALO, columns] = p_low[zh]
-        pq_ext[1, :, :HALO, columns] = pltpu.roll(p_low[zh], 4, 1)
-        pq_ext[0, :, HALO + rows :, columns] = p_high[zh]
-        pq_ext[1, :, HALO + rows :, columns] = pltpu.roll(p_high[zh], 4, 1)
+        for kd in range(2):
+            pq_ext[kd, :, :HALO, columns] = p_low[2 * kd + zh]
+            pq_ext[kd, :, HALO + rows :, columns] = p_high[2 * kd + zh]
     for kd in range(2):
         slopes = [slope(pq_ext, pq_z, (kd, f), rows, lanes) for f in range(fields)]
         for j in range(fields):
@@ -335,10 +384,9 @@
             buffer(fields, length // 2, 8, lanes), buffer(fields, length // 2, 8, lanes),
             buffer(2, fields, rows + 2 * HALO, lanes),
             buffer(2, fields, rows, half), buffer(2, fields, rows, half),
-            buffer(2, fields, 8, half), buffer(2, fields, 8, half),
-            buffer(2, fields, 8, half), buffer(2, fields, 8, half),
+            buffer(4, fields, 8, half), buffer(4, fields, 8, half),
             dma((4,)), dma((PIECES,)), dma((count_x,)), dma((count_x,)), dma((PIECES,)),
-            dma((3,)), dma((3,)), dma((3,)), dma((3,)),
+            dma((3,)), dma((3,)), dma((count_x + 1,)), dma((9,)),
         ],
         compiler_params=pltpu.CompilerParams(
             collective_id=0, has_side_effects=True, vmem_limit_bytes=24 * 2**20

time: 22.3 us -> 21.3 us (0.955)
  Pallas kernels: 22.1 us -> 21.1 us
    pallas_call x1, Pallas kernels: 21.2 us -> 20.2 us  [exchange(): pl.pallas_call(functools.partial(exchange_kernel, count_x, count_y, decay...]
where the time goes in v5:
time: 21.3 us; the launch traced here: 21.1 us
  Pallas kernels  21.1 us (99%)
    pallas_call x1, Pallas kernels, exchange(): pl.pallas_call(functools.partial(exchange_kernel, count_x, count_y, decay...  20.2 us
    pallas_call x1, Pallas kernels, finish(): pl.pallas_call(functools.partial(finish_kernel, decay), out_shape=jax.Sha...  0.93 us

profile of v5, /device:TPU:0, one launch (start us, length us, event | category | flops | bytes accessed | tf_op | source)
XLA Modules:
  0.0 21.1 jit_solution(18401738753411826015)
XLA Ops:
  0.0 20.2 %shard_map.46 = (f32[5,8,16,256]{3,2,1,0:T(8,128)S(1)}, f32[8,16,256]{2,1,0:T(8,128)S(1)}, f32[4,5,16,256]{3,2,1,0:T(8,128)S(1)}) custom-call(f32[5,8,16,256]{3,2,1,0:T(8,128)} %a_ref.1, f32[8,16,256]{2,1,0:T(8,128)} %mass_ref.1, f32[8,16,256]{2,1,0:T(8,128)} %level_ref.1, f32[5,5]{1,0:T(8,128)} %m_ref.1), custom_call_target="tpu_custom_call" | custom-call | tf_op jit(solution)/shard_map/pallas_call | solution.py:367
  20.2 0.9 %shard_map.47 = f32[5,8,16,256]{3,2,1,0:T(8,128)} custom-call(f32[5,8,16,256]{3,2,1,0:T(8,128)S(1)} %get-tuple-element.8.base, f32[8,16,256]{2,1,0:T(8,128)S(1)} %get-tuple-element.9.celerity, f32[4,5,16,256]{3,2,1,0:T(8,128)S(1)} %get-tuple-element.10.entering), custom_call_target="tpu_custom_call" | custom-call | tf_op jit(solution)/shard_map/pallas_call | solution.py:422

commit v6 on v5

--- a/solution.py
+++ b/solution.py
@@ -52,7 +52,7 @@
 def exchange_kernel(
     count_x, count_y, decay, scale,
     a_ref, mass_ref, level_ref, m_ref, base, celerity, entering,
-    a_v, mass, level, m, ends, own_in, own_out, pq, ext, u_edges, u_z, u_to_low, u_to_high,
+    a_v, mass, level, m, ends, own_in, own_out, own_halo, pq, ext, u_edges, u_z, u_to_low, u_to_high,
     u_low, u_high, pq_ext, pq_edges, pq_z, p_low, p_high,
     load_sem, send1, recv1, send2, recv2, send_u, recv_u, send_p, recv_p,
 ):
@@ -192,17 +192,23 @@
     to_low = jnp.logical_and(my_piece < 4, has_low)
     to_high = jnp.logical_and(my_piece >= 4, has_high)
 
+    def pack_halo(is_low):
+        for t in range(fields // 2):
+            own_halo[:, t] = packed(own_out[:, 2 * t], own_out[:, 2 * t + 1], is_low)
+        if fields % 2:
+            own_halo[:, fields // 2] = own_out[:, fields - 1]
+
     def low_copy(step):
         device = lax.rem(my_x + step, count_x)
         return remote(
-            own_out.at[device], p_high.at[slot], send_p.at[1 + step], recv_p.at[5 + slot],
+            own_halo.at[device], p_high.at[slot], send_p.at[1 + step], recv_p.at[5 + slot],
             {"gx": device, "gy": my_y - 1},
         )
 
     def high_copy(step):
         device = lax.rem(my_x + step, count_x)
         return remote(
-            own_out.at[device], p_low.at[slot], send_p.at[1 + step], recv_p.at[1 + slot],
+            own_halo.at[device], p_low.at[slot], send_p.at[1 + step], recv_p.at[1 + slot],
             {"gx": device, "gy": my_y + 1},
         )
 
@@ -232,11 +238,13 @@
 
         @pl.when(to_low)
         def _():
+            pack_halo(True)
             for step in far_first + [0]:
                 low_copy(step).start()
 
         @pl.when(to_high)
         def _():
+            pack_halo(False)
             for step in far_first + [0]:
                 high_copy(step).start()
 
@@ -333,7 +341,7 @@
     def _():
         for k in range(4):
             remote(
-                own_out.at[0], p_low.at[k], send_p.at[0], recv_p.at[1 + k],
+                own_halo.at[0], p_low.at[k], send_p.at[0], recv_p.at[1 + k],
                 {"gx": (4 + k) * stride, "gy": my_y - 1},
             ).wait_recv()
 
@@ -341,15 +349,19 @@
     def _():
         for k in range(4):
             remote(
-                own_out.at[0], p_high.at[k], send_p.at[0], recv_p.at[5 + k],
+                own_halo.at[0], p_high.at[k], send_p.at[0], recv_p.at[5 + k],
                 {"gx": k * stride, "gy": my_y + 1},
             ).wait_recv()
 
     for zh in range(2):
         columns = slice(zh * half, (zh + 1) * half)
         for kd in range(2):
-            pq_ext[kd, :, :HALO, columns] = p_low[2 * kd + zh]
-            pq_ext[kd, :, HALO + rows :, columns] = p_high[2 * kd + zh]
+            for f in range(fields):
+                below, above = p_low[2 * kd + zh, f // 2], p_high[2 * kd + zh, f // 2]
+                if f % 2:
+                    below, above = pltpu.roll(below, 4, 0), pltpu.roll(above, 4, 0)
+                pq_ext[kd, f, :HALO, columns] = below
+                pq_ext[kd, f, HALO + rows :, columns] = above
     for kd in range(2):
         slopes = [slope(pq_ext, pq_z, (kd, f), rows, lanes) for f in range(fields)]
         for j in range(fields):
@@ -377,6 +389,7 @@
             buffer(PIECES, fields, 8, half),
             buffer(count_x, fields, 8, half),
             buffer(count_x, fields, 8, half),
+            buffer(count_x, (fields + 1) // 2, 8, half),
             buffer(PIECES, fields, 8, half),
             buffer(fields, length, rows + 2 * HALO, lanes),
             buffer(fields, length, rows, half), buffer(fields, length, rows, half),
@@ -384,7 +397,7 @@
             buffer(fields, length // 2, 8, lanes), buffer(fields, length // 2, 8, lanes),
             buffer(2, fields, rows + 2 * HALO, lanes),
             buffer(2, fields, rows, half), buffer(2, fields, rows, half),
-            buffer(4, fields, 8, half), buffer(4, fields, 8, half),
+            buffer(4, (fields + 1) // 2, 8, half), buffer(4, (fields + 1) // 2, 8, half),
             dma((4,)), dma((PIECES,)), dma((count_x,)), dma((count_x,)), dma((PIECES,)),
             dma((3,)), dma((3,)), dma((count_x + 1,)), dma((9,)),
         ],

time: 21.3 us -> 20.8 us (0.977)
  Pallas kernels: 21.1 us -> 20.6 us
    pallas_call x1, Pallas kernels: 20.2 us -> 19.7 us  [exchange(): pl.pallas_call(functools.partial(exchange_kernel, count_x, count_y, decay...]
where the time goes in v6:
time: 20.8 us; the launch traced here: 20.6 us
  Pallas kernels  20.6 us (99%)
    pallas_call x1, Pallas kernels, exchange(): pl.pallas_call(functools.partial(exchange_kernel, count_x, count_y, decay...  19.7 us
    pallas_call x1, Pallas kernels, finish(): pl.pallas_call(functools.partial(finish_kernel, decay), out_shape=jax.Sha...  0.93 us

profile of v6, /device:TPU:0, one launch (start us, length us, event | category | flops | bytes accessed | tf_op | source)
XLA Modules:
  0.0 20.6 jit_solution(6291431204832441993)
XLA Ops:
  0.0 19.7 %shard_map.46 = (f32[5,8,16,256]{3,2,1,0:T(8,128)S(1)}, f32[8,16,256]{2,1,0:T(8,128)S(1)}, f32[4,5,16,256]{3,2,1,0:T(8,128)S(1)}) custom-call(f32[5,8,16,256]{3,2,1,0:T(8,128)} %a_ref.1, f32[8,16,256]{2,1,0:T(8,128)} %mass_ref.1, f32[8,16,256]{2,1,0:T(8,128)} %level_ref.1, f32[5,5]{1,0:T(8,128)} %m_ref.1), custom_call_target="tpu_custom_call" | custom-call | tf_op jit(solution)/shard_map/pallas_call | solution.py:379
  19.7 0.9 %shard_map.47 = f32[5,8,16,256]{3,2,1,0:T(8,128)} custom-call(f32[5,8,16,256]{3,2,1,0:T(8,128)S(1)} %get-tuple-element.8.base, f32[8,16,256]{2,1,0:T(8,128)S(1)} %get-tuple-element.9.celerity, f32[4,5,16,256]{3,2,1,0:T(8,128)S(1)} %get-tuple-element.10.entering), custom_call_target="tpu_custom_call" | custom-call | tf_op jit(solution)/shard_map/pallas_call | solution.py:435

commit v7 on v6

--- a/solution.py
+++ b/solution.py
@@ -54,7 +54,7 @@
     a_ref, mass_ref, level_ref, m_ref, base, celerity, entering,
     a_v, mass, level, m, ends, own_in, own_out, own_halo, pq, ext, u_edges, u_z, u_to_low, u_to_high,
     u_low, u_high, pq_ext, pq_edges, pq_z, p_low, p_high,
-    load_sem, send1, recv1, send2, recv2, send_u, recv_u, send_p, recv_p,
+    load_sem, send1, recv1, send2, recv2, send_u, recv_u, send_p, recv_p, send_z, recv_z,
 ):
     fields, length, rows, lanes = a_v.shape
     half = lanes // 2
@@ -288,22 +288,29 @@
 
     lax.fori_loop(0, length, plane, 0)
 
-    for piece in range(PIECES):
-        arrived = remote(
-            own_out.at[0], pq.at[piece], send2.at[0], recv2.at[piece], {"gx": piece * stride}
-        )
-        pl.when(piece * stride != my_x)(arrived.wait_recv)
-
-    for kd in range(2):
-        for yh in range(2):
-            piece = yh * 4 + kd * 2
-            pq_edges[kd, :, yh * 8 : yh * 8 + 8, :] = edges(pq[piece], pq[piece + 1])
+    last = []
+    for yh in range(2):
+        for kd in range(2):
+            first = yh * 4 + kd * 2
+            at = slice(yh * 8, yh * 8 + 8)
+            for piece in (first, first + 1):
+                arrived = remote(
+                    own_out.at[0], pq.at[piece], send2.at[0], recv2.at[piece],
+                    {"gx": piece * stride},
+                )
+                pl.when(piece * stride != my_x)(arrived.wait_recv)
+            pq_edges[kd, :, at, :] = edges(pq[first], pq[first + 1])
+            last.append(
+                remote(
+                    pq_edges.at[kd, :, at, :], pq_z.at[kd, :, at, :],
+                    send_z.at[yh * 2 + kd], recv_z.at[yh * 2 + kd], other,
+                )
+            )
+            last[-1].start()
             for zh in range(2):
                 pq_ext[
                     kd, :, HALO + yh * 8 : HALO + yh * 8 + 8, zh * half : (zh + 1) * half
-                ] = pq[piece + zh]
-    copy_pz = remote(pq_edges, pq_z, send_p.at[0], recv_p.at[0], other)
-    copy_pz.start()
+                ] = pq[first + zh]
     entering[0:2] = pq_ext[:, :, HALO : HALO + rows, :]
 
     for step in steps:
@@ -335,7 +342,8 @@
     else:
         pl.when(owner)(sent)
 
-    copy_pz.wait()
+    for copy in last:
+        copy.wait()
 
     @pl.when(has_low)
     def _():
@@ -400,6 +408,7 @@
             buffer(4, (fields + 1) // 2, 8, half), buffer(4, (fields + 1) // 2, 8, half),
             dma((4,)), dma((PIECES,)), dma((count_x,)), dma((count_x,)), dma((PIECES,)),
             dma((3,)), dma((3,)), dma((count_x + 1,)), dma((9,)),
+            dma((4,)), dma((4,)),
         ],
         compiler_params=pltpu.CompilerParams(
             collective_id=0, has_side_effects=True, vmem_limit_bytes=24 * 2**20

time: 20.8 us -> 20.8 us (level)
  no operation moved by 1% of the time
where the time goes in v7:
time: 20.8 us; the launch traced here: 20.6 us
  Pallas kernels  20.6 us (99%)
    pallas_call x1, Pallas kernels, exchange(): pl.pallas_call(functools.partial(exchange_kernel, count_x, count_y, decay...  19.7 us
    pallas_call x1, Pallas kernels, finish(): pl.pallas_call(functools.partial(finish_kernel, decay), out_shape=jax.Sha...  0.93 us

profile of v7, /device:TPU:0, one launch (start us, length us, event | category | flops | bytes accessed | tf_op | source)
XLA Modules:
  0.0 20.6 jit_solution(9531966036449015813)
XLA Ops:
  0.0 19.7 %shard_map.46 = (f32[5,8,16,256]{3,2,1,0:T(8,128)S(1)}, f32[8,16,256]{2,1,0:T(8,128)S(1)}, f32[4,5,16,256]{3,2,1,0:T(8,128)S(1)}) custom-call(f32[5,8,16,256]{3,2,1,0:T(8,128)} %a_ref.1, f32[8,16,256]{2,1,0:T(8,128)} %mass_ref.1, f32[8,16,256]{2,1,0:T(8,128)} %level_ref.1, f32[5,5]{1,0:T(8,128)} %m_ref.1), custom_call_target="tpu_custom_call" | custom-call | tf_op jit(solution)/shard_map/pallas_call | solution.py:387
  19.7 0.9 %shard_map.47 = f32[5,8,16,256]{3,2,1,0:T(8,128)} custom-call(f32[5,8,16,256]{3,2,1,0:T(8,128)S(1)} %get-tuple-element.8.base, f32[8,16,256]{2,1,0:T(8,128)S(1)} %get-tuple-element.9.celerity, f32[4,5,16,256]{3,2,1,0:T(8,128)S(1)} %get-tuple-element.10.entering), custom_call_target="tpu_custom_call" | custom-call | tf_op jit(solution)/shard_map/pallas_call | solution.py:444
